TPU v7x, 32 devices: a whole 2x2x4 slice. The times are simulated.
32 devices in a mesh: segment: 8 (over z, core), node: 4 (over y, x).
Axes of the slice: x: 2, y: 2, z: 4, core: 2. Of those that a mesh axis runs over, the one named last changes fastest.
Arguments:
- features: bfloat16 [2, 2048, 256], P(None, 'node'), may hold values from -6 to 6
- tiles: bfloat16 [2, 16, 8, 128, 128], P(None, 'node'), may hold values from -0.25 to 0.25
- tile_cols: int32 [2, 16, 8], P(None, 'node'), may hold values from 0 to 15, as said below
- tile_count: int32 [2, 16], P(None, 'node'), may hold values from 1 to 8
- weights: bfloat16 [8, 256, 256], P('segment'), may hold values from -0.375 to 0.375
Outputs:
- layer_outputs: bfloat16 [8, 2, 2048, 256], P('segment', None, 'node')
Inputs may be any that keep to these rules, and one draw needn't show every extreme that they name: `tile_cols`: with P = 4 block rows per node group of 512 nodes, the block column of a tile in block row b lies in group g - 1, g or g + 1 (counted modulo 2048 / 512 groups) where g = b // P is the group of b. `tile_count`: slots from the count on are padding.
All inputs are finite; a program needn't handle non-finite values.
Results may differ from a plain program's by a relative error of at most 0.011.
Values may be sent and summed in bfloat16 or wider, within the bound.
A program may use at most 64 MiB of HBM per device.

v0:
```python
import jax
import jax.numpy as jnp
import numpy as np
from jax import lax
from jax.experimental import pallas as pl
from jax.experimental.pallas import tpu as pltpu
from jax.sharding import PartitionSpec as P


def with_halo(array, sides, width):
    for axis, dim in sides:
        count, length = (lax.axis_size(axis), array.shape[dim])
        up = [(i, (i + 1) % count) for i in range(count)]
        down = [(j, i) for i, j in up]
        last = lax.slice_in_dim(array, length - width, length, axis=dim)
        first = lax.slice_in_dim(array, 0, width, axis=dim)
        before = lax.ppermute(last, axis, up)
        after = lax.ppermute(first, axis, down)
        array = jnp.concatenate([before, array, after], axis=dim)
    return array


def passed_along(block, axis, distance):
    devices = range(lax.axis_size(axis))
    route = [(i - distance, i) for i in devices if i - distance in devices]
    return lax.ppermute(block, axis, route)


def layer_rows(window, masked, columns, initial, weight, beta_mix):
    tile_size = masked.shape[-1]
    feature_width = window.shape[-1]
    grouped = window.reshape(window.shape[0] // tile_size, tile_size, feature_width)
    picked = grouped[columns]
    aggregate = jnp.einsum("bkij,bkjd->bid", masked, picked, preferred_element_type=jnp.float32)
    aggregate = aggregate.reshape(-1, feature_width)
    support = (0.9 * aggregate + 0.1 * initial.astype(jnp.float32)).astype(jnp.bfloat16)
    branch = jnp.dot(support, weight, preferred_element_type=jnp.float32)
    combined = (1.0 - beta_mix) * support.astype(jnp.float32) + beta_mix * branch
    return jnp.maximum(combined, 0.0).astype(jnp.bfloat16)


def on_device(features, tiles, tile_cols, tile_count, weights):
    segments = lax.axis_size("segment")
    groups = lax.axis_size("node")
    segment_id = lax.axis_index("segment")
    group_id = lax.axis_index("node")
    spans = features.shape[0]
    per_group = tiles.shape[1]
    total_blocks = per_group * groups
    first_block = (group_id - 1) * per_group
    local_cols = (tile_cols - first_block + total_blocks) % total_blocks
    slot_ids = jnp.arange(tiles.shape[2], dtype=jnp.int32)
    live = (slot_ids[None, None, :] < tile_count[:, :, None]).astype(jnp.bfloat16)
    masked = tiles * live[:, :, :, None, None]
    beta_mix = jnp.log(0.5 / (segment_id.astype(jnp.float32) + 1.0) + 1.0)
    weight = weights[0]
    rows_here = features.shape[1]

    def step(step_no, state_pair):
        incoming, stored = state_pair
        offset_now = step_no - segment_id
        active = (offset_now >= 0) & (offset_now < spans)
        span_id = jnp.clip(offset_now, 0, spans - 1)
        initial = lax.dynamic_index_in_dim(features, span_id, 0, keepdims=False)
        layer_input = jnp.where(segment_id == 0, initial, incoming)
        window = with_halo(layer_input, (("node", 0),), rows_here)
        span_tiles = lax.dynamic_index_in_dim(masked, span_id, 0, keepdims=False)
        span_cols = lax.dynamic_index_in_dim(local_cols, span_id, 0, keepdims=False)
        result = layer_rows(window, span_tiles, span_cols, initial, weight, beta_mix)
        updated = lax.dynamic_update_index_in_dim(stored, result, span_id, 0)
        stored = jnp.where(active, updated, stored)
        incoming = passed_along(result, "segment", 1)
        return (incoming, stored)

    start_pair = (
        jnp.zeros(features.shape[1:], jnp.bfloat16),
        jnp.zeros(features.shape, jnp.bfloat16),
    )
    final_pair = lax.fori_loop(0, segments + spans - 1, step, start_pair)
    stored = final_pair[1]
    return stored[None]


MESH = pl.DeviceIdType.MESH
ROWS = 512
WIDE = 12


def whole_kernel(betas, tiles, feats, cols, counts, weight, out,
                 a_all, f_all, c_vm, n_vm, c_all, n_all, w_all, dense, hid, own_ref, send_ref,
                 loc, asem, arec, fsem, frec, csem, crec, nsem, nrec, wsem, wrec, osem, orec):
    seg = lax.axis_index("segment")
    g = lax.axis_index("node")
    c = seg % 2
    z = seg // 2
    span = z % 2
    xn = g + 1 - 2 * (g % 2)
    yn = (g + 2) % 4
    dn = 3 - g
    partner = (z + 1 - 2 * span) * 2 + c
    last = seg + 2 - 2 * span

    def at(start, size):
        return pl.ds(pl.multiple_of(start, size), size)

    def remote(src, dst, ssem, rsem, dev):
        return pltpu.make_async_remote_copy(src, dst, ssem, rsem, device_id=dev, device_id_type=MESH)

    barrier = pltpu.get_barrier_semaphore()
    for n in (xn, yn, dn):
        pl.semaphore_signal(barrier, inc=1, device_id={"node": n}, device_id_type=MESH)
    for d in range(1, 8):
        pl.semaphore_signal(barrier, inc=1, device_id={"segment": (seg + d) % 8}, device_id_type=MESH)
    pl.semaphore_wait(barrier, 10)

    local = [pltpu.make_async_copy(s, t, loc.at[k]) for k, (s, t) in enumerate((
        (cols, c_vm.at[g]), (counts, n_vm.at[g]), (feats.at[span], f_all.at[g]),
        (tiles.at[span], a_all.at[g]), (weight.at[0], w_all.at[seg])))]
    for cp in local:
        cp.start()

    small = []
    for d, n in enumerate((xn, yn, dn)):
        small.append(remote(cols, c_vm.at[g], csem.at[d], crec.at[d], {"node": n}))
        small.append(remote(counts, n_vm.at[g], nsem.at[d], nrec.at[d], {"node": n}))
    first = [remote(feats.at[span], f_all.at[g], fsem.at[d], frec.at[d], {"node": n})
             for d, n in enumerate((xn, yn, dn))]
    for cp in small + first:
        cp.start()

    low_copies = [remote(weight.at[0], w_all.at[seg], wsem.at[d], wrec.at[seg], {"segment": (seg + d + 1) % 8})
                  for d in range(7)]
    high_copies = [remote(weight.at[0], w_all.at[seg], wsem.at[d], wrec.at[seg], {"segment": 4 + (seg + d + 1) % 4})
                   for d in range(3)]

    @pl.when(z < 2)
    def _():
        for cp in low_copies:
            cp.start()

    def half(h):
        return pl.ds(h * 2, 2)

    def from_here(h, k, n):
        return remote(tiles.at[span, half(h)], a_all.at[g, half(h)], asem.at[k], arec.at[k], {"node": n})

    x0, y1, x1, y0 = from_here(0, 0, xn), from_here(1, 1, yn), from_here(1, 2, xn), from_here(0, 3, yn)
    for cp in (x0, y1, x1, y0):
        cp.start()

    @pl.when(z >= 2)
    def _():
        for cp in high_copies:
            cp.start()

    for cp in local:
        cp.wait()
    for cp in small:
        cp.wait()
    meta = [pltpu.make_async_copy(c_vm, c_all, loc.at[0]), pltpu.make_async_copy(n_vm, n_all, loc.at[1])]
    for cp in meta:
        cp.start()
    for cp in meta:
        cp.wait()

    def densify(grp, h):
        def block(i, carry):
            row = h * 2 + i
            live = counts_of(grp, row)
            place = [(c_all[grp, span, row, k] - 4 * (grp - 1) + 16) % 16 for k in range(8)]
            place = [jnp.where(k < live, place[k], -1) for k in range(8)]

            def strip(r, carry):
                rows = at(r * 32, 32)
                part = [a_all[grp, row, k, rows, :].astype(jnp.float32) for k in range(8)]
                for j in range(WIDE):
                    total = None
                    for k in range(8):
                        term = part[k] * jnp.where(place[k] == j, 1.0, 0.0)
                        total = term if total is None else total + term
                    dense[grp * 4 + row, rows, j * 128:(j + 1) * 128] = total.astype(jnp.bfloat16)
                return carry

            return lax.fori_loop(0, 4, strip, carry)

        lax.fori_loop(0, 2, block, 0)

    def counts_of(grp, row):
        return n_all[grp, span, row]

    densify(g, 0)
    densify(g, 1)

    via = xn * (1 - c) + yn * c
    beyond = yn * (1 - c) + xn * c
    peer = seg + 1 - 2 * c
    arrived_at = remote(tiles.at[span, half(0)], a_all.at[g, half(0)], asem.at[c], arec.at[c], {"node": xn})
    other_at = remote(tiles.at[span, half(0)], a_all.at[g, half(0)], asem.at[1 - c], arec.at[1 - c], {"node": xn})
    arrived_at.wait_recv()
    onward = [remote(a_all.at[via, 2 * c + i], a_all.at[via, 2 * c + i], asem.at[4 + i], arec.at[4 + i],
                     {"node": beyond}) for i in range(2)]
    for cp in onward:
        cp.start()
    other_at.wait_recv()
    densify(xn, 0)
    densify(yn, 1)

    def put(buf, grp, value):
        hid[buf, at((grp + 1) * ROWS, ROWS), :] = value

        @pl.when(grp == 3)
        def _():
            hid[buf, 0:ROWS, :] = value

        @pl.when(grp == 0)
        def _():
            hid[buf, 5 * ROWS:6 * ROWS, :] = value

    for cp in first:
        cp.wait()

    def start(grp, carry):
        put(0, grp, f_all[grp])
        return carry

    lax.fori_loop(0, 4, start, 0)
    x1.wait_recv()
    densify(xn, 1)
    y0.wait_recv()
    densify(yn, 0)
    shares = []
    for i in range(2):
        onward[i].wait_recv()
        p = a_all.at[dn, 2 * c + i]
        shares.append(remote(p, p, asem.at[6 + i], arec.at[6 + i], {"segment": peer}))
        shares[i].start()

    def weight_here(l):
        @pl.when(l != seg)
        def _():
            remote(weight.at[0], w_all.at[l], wsem.at[0], wrec.at[l], {"segment": peer}).wait_recv()

    def group_rows(l, grp, window):
        lhs = dense[pl.ds(grp * 4, 4)].reshape(ROWS, WIDE * 128)
        agg = jnp.dot(lhs, window, preferred_element_type=jnp.float32)
        sup = (0.9 * agg + 0.1 * f_all[grp].astype(jnp.float32)).astype(jnp.bfloat16)
        branch = jnp.dot(sup, w_all[l], preferred_element_type=jnp.float32)
        beta = betas[l]
        res = (1.0 - beta) * sup.astype(jnp.float32) + beta * branch
        return jnp.maximum(res, 0.0).astype(jnp.bfloat16)

    def window_of(buf, grp):
        return hid[buf, pl.ds(pl.multiple_of(grp * ROWS, ROWS), 3 * ROWS), :]

    def layer(l, carry):
        cur = l % 2
        weight_here(l)

        def one(grp, carry):
            put(1 - cur, grp, group_rows(l, grp, window_of(cur, grp)))
            return carry

        return lax.fori_loop(0, 4, one, carry)

    weight_here(0)

    def early(i, carry):
        grp = (dn + 1 + i) % 4
        put(1, grp, group_rows(0, grp, window_of(0, grp)))
        return carry

    lax.fori_loop(0, 3, early, 0)
    densify(dn, c)
    for cp in shares:
        cp.wait_recv()
    densify(dn, 1 - c)
    put(1, dn, group_rows(0, dn, window_of(0, dn)))
    lax.fori_loop(1, last - 1, layer, 0)
    cur = (last - 1) % 2
    low_at = at((g + 1) * ROWS, ROWS)
    across = remote(send_ref, out.at[0, span], osem, orec, {"segment": partner})

    @pl.when(span == 1)
    def _():
        send_ref[...] = hid[cur, low_at, :]
        across.start()

    @pl.when(span == 0)
    def _():
        own_ref[...] = hid[cur, low_at, :]

    weight_here(last - 1)

    def near(i, carry):
        grp = (g + 3 + i) % 4
        hid[1 - cur, at(i * ROWS, ROWS), :] = group_rows(last - 1, grp, window_of(cur, grp))
        return carry

    lax.fori_loop(0, 3, near, 0)
    weight_here(last)
    high = group_rows(last, g, hid[1 - cur, 0:3 * ROWS, :])

    @pl.when(span == 0)
    def _():
        send_ref[...] = high
        across.start()

    @pl.when(span == 1)
    def _():
        own_ref[...] = high

    mine = pltpu.make_async_copy(own_ref, out.at[0, span], loc.at[0])
    mine.start()

    def rest(l, carry):
        weight_here(l)
        return carry

    lax.fori_loop(last + 1, jnp.where(z < 2, 4, 8), rest, 0)
    for cp in [x0, y1, x1, y0] + onward + shares:
        cp.wait_send()

    @pl.when(z < 2)
    def _():
        for cp in low_copies:
            cp.wait_send()

    @pl.when(z >= 2)
    def _():
        for cp in high_copies:
            cp.wait_send()

    mine.wait()
    across.wait()


def whole_spans(features, tiles, tile_cols, tile_count, weights):
    hbm = pl.BlockSpec(memory_space=pltpu.HBM)
    bf = jnp.bfloat16
    dma = pltpu.SemaphoreType.DMA
    betas = jnp.asarray(np.log(0.5 / (np.arange(8, dtype=np.float32) + 1.0) + 1.0), jnp.float32)
    width = features.shape[-1]
    return pl.pallas_call(
        whole_kernel,
        out_shape=jax.ShapeDtypeStruct((1,) + features.shape, bf),
        in_specs=[pl.BlockSpec(memory_space=pltpu.SMEM)] + [hbm] * 5,
        out_specs=hbm,
        scratch_shapes=[
            pltpu.VMEM((4,) + tiles.shape[1:], bf),
            pltpu.VMEM((4,) + features.shape[1:], bf),
            pltpu.VMEM((4,) + tile_cols.shape, jnp.int32),
            pltpu.VMEM((4,) + tile_count.shape, jnp.int32),
            pltpu.SMEM((4,) + tile_cols.shape, jnp.int32),
            pltpu.SMEM((4,) + tile_count.shape, jnp.int32),
            pltpu.VMEM((8,) + weights.shape[1:], bf),
            pltpu.VMEM((16, 128, WIDE * 128), bf),
            pltpu.VMEM((2, 6 * ROWS, width), bf),
            pltpu.VMEM((ROWS, width), bf),
            pltpu.VMEM((ROWS, width), bf),
            dma((5,)), dma((8,)), dma((8,)), dma((3,)), dma((3,)), dma((3,)), dma((3,)),
            dma((3,)), dma((3,)), dma((7,)), dma((8,)), dma, dma,
        ],
        compiler_params=pltpu.CompilerParams(collective_id=0, has_side_effects=True,
                                             vmem_limit_bytes=63 * 1024 * 1024),
        cost_estimate=pl.CostEstimate(flops=15_000_000_000, bytes_accessed=8_000_000, transcendentals=0),
        name="whole",
    )(betas, tiles, features, tile_cols, tile_count, weights)


def solution(mesh):
    in_specs = (
        P(None, "node", None),
        P(None, "node", None, None, None),
        P(None, "node", None),
        P(None, "node"),
        P("segment", None, None),
    )
    out_specs = P("segment", None, "node", None)
    small = mesh.shape["segment"] == 8 and mesh.shape["node"] == 4
    return jax.shard_map(
        whole_spans if small else on_device, mesh=mesh, in_specs=in_specs, out_specs=out_specs, check_vma=False
    )
```

profile of v0, /device:TPU:25, one launch (start us, length us, event | category | flops | bytes accessed | tf_op | source)
XLA Modules:
  0.0 76.0 jit_solution(458785556101949028)
XLA Ops:
  0.0 74.1 %whole.1 = bf16[1,2,512,256]{3,2,1,0:T(8,128)(2,1)} custom-call(f32[8]{0:T(128)} %constant.2.clone.betas, bf16[2,4,8,128,128]{4,3,2,1,0:T(8,128)(2,1)} %tiles.1, bf16[2,512,256]{2,1,0:T(8,128)(2,1)} %feats.1, s32[2,4,8]{2,1,0:T(4,128)} %cols.1, s32[2,4]{1,0:T(2,128)} %counts.1, bf16[1,256,256]{2,1,0:T(8,128)(2,1)} %weight.1), custom_call_target="tpu_custom_call" | custom-call | flops 15000000512 | bytes 8000000 | tf_op jit(solution)/shard_map/whole/pallas_call | solution.py:343
  74.1 1.9 %copy.8 = bf16[1,2,512,256]{3,2,1,0:T(8,128)(2,1)} copy(bf16[1,2,512,256]{3,2,1,0:T(8,128)(2,1)} %whole.1) | data formatting | bytes 1048576
where the time goes:
time: 76.2 us; the launch traced here: 76 us
  Pallas kernels  74.1 us (97%)
  local copies, waits for them, and re-layouts  1.87 us (2%)
    pallas_call x1, Pallas kernels, whole_spans(): pl.pallas_call(whole_kernel, out_shape=jax.ShapeDtypeStruct((1,) + featur...  74.1 us
    unnamed x1, local copies, waits for them, and re-layouts  1.87 us

commit v1 on v0

--- a/solution.py
+++ b/solution.py
@@ -124,7 +124,9 @@
         small.append(remote(cols, c_vm.at[g], csem.at[d], crec.at[d], {"node": n}))
         small.append(remote(counts, n_vm.at[g], nsem.at[d], nrec.at[d], {"node": n}))
     first = [remote(feats.at[span], f_all.at[g], fsem.at[d], frec.at[d], {"node": n})
-             for d, n in enumerate((xn, yn, dn))]
+             for d, n in enumerate((xn, yn))]
+    part = at(c * 256, 256)
+    first.append(remote(feats.at[span, part], f_all.at[g, part], fsem.at[2], frec.at[2], {"node": dn}))
     for cp in small + first:
         cp.start()
 
@@ -138,14 +140,11 @@
         for cp in low_copies:
             cp.start()
 
-    def half(h):
-        return pl.ds(h * 2, 2)
-
-    def from_here(h, k, n):
-        return remote(tiles.at[span, half(h)], a_all.at[g, half(h)], asem.at[k], arec.at[k], {"node": n})
-
-    x0, y1, x1, y0 = from_here(0, 0, xn), from_here(1, 1, yn), from_here(1, 2, xn), from_here(0, 3, yn)
-    for cp in (x0, y1, x1, y0):
+    front = pl.ds(2 * c, 2)
+    inner = pl.ds(2 - c, 1)
+    direct = [remote(tiles.at[span, rows], a_all.at[g, rows], asem.at[k], arec.at[k], {"node": n})
+              for k, (rows, n) in enumerate(((front, xn), (front, yn), (inner, xn), (inner, yn)))]
+    for cp in direct:
         cp.start()
 
     @pl.when(z >= 2)
@@ -163,9 +162,9 @@
     for cp in meta:
         cp.wait()
 
-    def densify(grp, h):
+    def densify(grp, from_row, count):
         def block(i, carry):
-            row = h * 2 + i
+            row = from_row + i
             live = counts_of(grp, row)
             place = [(c_all[grp, span, row, k] - 4 * (grp - 1) + 16) % 16 for k in range(8)]
             place = [jnp.where(k < live, place[k], -1) for k in range(8)]
@@ -183,27 +182,36 @@
 
             return lax.fori_loop(0, 4, strip, carry)
 
-        lax.fori_loop(0, 2, block, 0)
+        lax.fori_loop(0, count, block, 0)
 
     def counts_of(grp, row):
         return n_all[grp, span, row]
 
-    densify(g, 0)
-    densify(g, 1)
+    densify(g, 0, 4)
 
     via = xn * (1 - c) + yn * c
     beyond = yn * (1 - c) + xn * c
     peer = seg + 1 - 2 * c
-    arrived_at = remote(tiles.at[span, half(0)], a_all.at[g, half(0)], asem.at[c], arec.at[c], {"node": xn})
-    other_at = remote(tiles.at[span, half(0)], a_all.at[g, half(0)], asem.at[1 - c], arec.at[1 - c], {"node": xn})
-    arrived_at.wait_recv()
-    onward = [remote(a_all.at[via, 2 * c + i], a_all.at[via, 2 * c + i], asem.at[4 + i], arec.at[4 + i],
-                     {"node": beyond}) for i in range(2)]
-    for cp in onward:
-        cp.start()
-    other_at.wait_recv()
-    densify(xn, 0)
-    densify(yn, 1)
+
+    def across_chip(piece, k):
+        return remote(piece, piece, asem.at[k], arec.at[k], {"segment": peer})
+
+    for cp in first:
+        cp.wait_recv()
+    first_share = across_chip(f_all.at[dn, part], 10)
+    first_share.start()
+    for k in (c, 1 - c):
+        remote(tiles.at[span, front], a_all.at[g, front], asem.at[k], arec.at[k], {"node": xn}).wait_recv()
+        if k is c:
+            onward = [remote(a_all.at[via, 2 * c + i], a_all.at[via, 2 * c + i], asem.at[4 + i], arec.at[4 + i],
+                             {"node": beyond}) for i in range(2)]
+            for cp in onward:
+                cp.start()
+    edge = [across_chip(a_all.at[n, 3 * c], 8 + k) for k, n in enumerate((xn, yn))]
+    for cp in edge:
+        cp.start()
+    densify(xn, 2 * c, 2)
+    densify(yn, 2 * c, 2)
 
     def put(buf, grp, value):
         hid[buf, at((grp + 1) * ROWS, ROWS), :] = value
@@ -216,18 +224,21 @@
         def _():
             hid[buf, 5 * ROWS:6 * ROWS, :] = value
 
-    for cp in first:
-        cp.wait()
+    first_share.wait_recv()
 
     def start(grp, carry):
         put(0, grp, f_all[grp])
         return carry
 
     lax.fori_loop(0, 4, start, 0)
-    x1.wait_recv()
-    densify(xn, 1)
-    y0.wait_recv()
-    densify(yn, 0)
+    direct[2].wait_recv()
+    densify(xn, 2 - c, 1)
+    direct[3].wait_recv()
+    densify(yn, 2 - c, 1)
+    edge[0].wait_recv()
+    densify(xn, 3 - 3 * c, 1)
+    edge[1].wait_recv()
+    densify(yn, 3 - 3 * c, 1)
     shares = []
     for i in range(2):
         onward[i].wait_recv()
@@ -270,10 +281,10 @@
         return carry
 
     lax.fori_loop(0, 3, early, 0)
-    densify(dn, c)
+    densify(dn, 2 * c, 2)
     for cp in shares:
         cp.wait_recv()
-    densify(dn, 1 - c)
+    densify(dn, 2 - 2 * c, 2)
     put(1, dn, group_rows(0, dn, window_of(0, dn)))
     lax.fori_loop(1, last - 1, layer, 0)
     cur = (last - 1) % 2
@@ -317,7 +328,7 @@
         return carry
 
     lax.fori_loop(last + 1, jnp.where(z < 2, 4, 8), rest, 0)
-    for cp in [x0, y1, x1, y0] + onward + shares:
+    for cp in direct + onward + shares + edge + first + [first_share]:
         cp.wait_send()
 
     @pl.when(z < 2)
@@ -357,7 +368,7 @@
             pltpu.VMEM((2, 6 * ROWS, width), bf),
             pltpu.VMEM((ROWS, width), bf),
             pltpu.VMEM((ROWS, width), bf),
-            dma((5,)), dma((8,)), dma((8,)), dma((3,)), dma((3,)), dma((3,)), dma((3,)),
+            dma((5,)), dma((11,)), dma((11,)), dma((3,)), dma((3,)), dma((3,)), dma((3,)),
             dma((3,)), dma((3,)), dma((7,)), dma((8,)), dma, dma,
         ],
         compiler_params=pltpu.CompilerParams(collective_id=0, has_side_effects=True,

time: 76.2 us -> 67.8 us (0.89)
  Pallas kernels: 74.1 us -> 65.8 us
    pallas_call x1, Pallas kernels: 74.1 us -> 65.8 us  [whole_spans(): pl.pallas_call(whole_kernel, out_shape=jax.ShapeDtypeStruct((1,) + featur...]
where the time goes in v1:
time: 67.8 us; the launch traced here: 67.6 us
  Pallas kernels  65.8 us (97%)
  local copies, waits for them, and re-layouts  1.87 us (3%)
    pallas_call x1, Pallas kernels, whole_spans(): pl.pallas_call(whole_kernel, out_shape=jax.ShapeDtypeStruct((1,) + featur...  65.8 us
    unnamed x1, local copies, waits for them, and re-layouts  1.87 us

profile of v1, /device:TPU:25, one launch (start us, length us, event | category | flops | bytes accessed | tf_op | source)
XLA Modules:
  0.0 67.6 jit_solution(3077716027227020425)
XLA Ops:
  0.0 65.8 %whole.1 = bf16[1,2,512,256]{3,2,1,0:T(8,128)(2,1)} custom-call(f32[8]{0:T(128)} %constant.2.clone.betas, bf16[2,4,8,128,128]{4,3,2,1,0:T(8,128)(2,1)} %tiles.1, bf16[2,512,256]{2,1,0:T(8,128)(2,1)} %feats.1, s32[2,4,8]{2,1,0:T(4,128)} %cols.1, s32[2,4]{1,0:T(2,128)} %counts.1, bf16[1,256,256]{2,1,0:T(8,128)(2,1)} %weight.1), custom_call_target="tpu_custom_call" | custom-call | flops 15000000512 | bytes 8000000 | tf_op jit(solution)/shard_map/whole/pallas_call | solution.py:354
  65.8 1.9 %copy.8 = bf16[1,2,512,256]{3,2,1,0:T(8,128)(2,1)} copy(bf16[1,2,512,256]{3,2,1,0:T(8,128)(2,1)} %whole.1) | data formatting | bytes 1048576
